TPU v7x, 32 devices: a whole 2x2x4 slice. The times are simulated.
32 devices in a mesh: group: 2 (over y), replica: 4 (over x, core), tensor: 4 (over z).
Axes of the slice: x: 2, y: 2, z: 4, core: 2. Of those that a mesh axis runs over, the one named last changes fastest.
Arguments:
- tokens: bfloat16 [8, 2, 128, 8192], P(('group', 'replica'), None, None, 'tensor'), parts along dimension 0, may hold values from -6 to 6
- merged_query: bfloat16 [8, 8192, 4096], P(('group', 'replica'), None, 'tensor'), parts along dimension 0, may hold values from -0.0625 to 0.0625
- merged_output: bfloat16 [8, 4096, 8192], P(('group', 'replica'), 'tensor'), parts along dimension 0, may hold values from -0.125 to 0.125
- store_wide: bfloat16 [8, 8, 2, 32, 8192], P(('group', 'replica'), None, None, None, 'tensor'), parts along dimension 0, may hold values from -0.59765625 to 0.59765625
- store_narrow: bfloat16 [8, 8, 2, 32, 4096], P(('group', 'replica'), None, None, None, 'tensor'), parts along dimension 0, may hold values from -0.59765625 to 0.59765625
- key_cache: bfloat16 [8, 4, 128, 48, 128], P(('group', 'replica'), 'tensor'), parts along dimension 0, may hold values from -600 to 600, as said below
- value_cache: bfloat16 [8, 4, 128, 48, 128], P(('group', 'replica'), 'tensor'), parts along dimension 0, may hold values from -6 to 6, as said below
- context_length: int32 [8, 128], P(('group', 'replica')), parts along dimension 0, may hold values from 2 to 47
- owner_slot: int32 [32], P('group'), parts along dimension 0, may hold values from 0 to 31, as said below
- old_tenant: int32 [8], P('group'), parts along dimension 0, may hold values from 0 to 15
- new_tenant: int32 [8], P('group'), parts along dimension 0, may hold values from 0 to 15
Outputs:
- attention_out: bfloat16 [8, 2, 128, 8192], P(('group', 'replica'), None, None, 'tensor'), parts along dimension 0
There are 2 independent parts, one for each index of `group`. A program takes and returns all parts, laid end to end along the dimension named above; each array names one. Nothing has to cross between parts.
Inputs may be any that keep to these rules, and one draw needn't show every extreme that they name: `owner_slot`: all values differ; a tenant's adapter lies in replica value // 8, slot value % 8. `key_cache`: entries [j, t] and [j, u] are equal where t == u. `value_cache`: entries [j, t] and [j, u] are equal where t == u.
All inputs are finite; a program needn't handle non-finite values.
Results may differ from a plain program's by a relative error of at most 0.015.
The roundings to bfloat16 on the way count: a program that leaves them out, or rounds other values in their place, can miss the bound.
Values may be sent and summed in bfloat16 or wider, within the bound.
A program may use at most 256 MiB of HBM per device.

v0:
```python
import jax
import jax.numpy as jnp
from jax import lax
from jax.sharding import PartitionSpec as P

adapter_scale = 0.25


def outer_product(left_factor, right_factor):
    return lax.dot_general(
        left_factor, right_factor, (((0,), (0,)), ((), ())), preferred_element_type=jnp.float32
    )


def attend(queries, key_rows, value_rows, visible):
    row_count, place_count, head_size = key_rows.shape
    head_count = queries.shape[1] // head_size
    shaped = queries.reshape(row_count, head_count, head_size)
    scores = jnp.einsum(
        "rqd,rcd->qrc", shaped, key_rows, preferred_element_type=jnp.float32
    ) * head_size ** (-0.5)
    scores = jnp.where(visible[None], scores, -jnp.inf)
    highest = jnp.max(scores, axis=2, keepdims=True)
    weights = jnp.exp(scores - highest)
    probability = (weights / jnp.sum(weights, axis=2, keepdims=True)).astype(jnp.bfloat16)
    blended = jnp.einsum(
        "qrc,rcd->rqd", probability, value_rows, preferred_element_type=jnp.float32
    )
    return blended.astype(jnp.bfloat16).reshape(row_count, head_count * head_size)


def on_device(
    tokens,
    merged_query,
    merged_output,
    store_wide,
    store_narrow,
    key_cache,
    value_cache,
    context_length,
    owner_slot,
    old_tenant,
    new_tenant,
):
    slot_count = store_wide.shape[1]
    rank_count = store_wide.shape[3]
    local_width = store_wide.shape[4]
    narrow_width = store_narrow.shape[4]
    wide_span = 2 * rank_count * local_width
    narrow_span = 2 * rank_count * narrow_width
    my_replica = lax.axis_index("replica")
    wanted = jnp.stack([owner_slot[old_tenant], owner_slot[new_tenant]], axis=1)
    owner_rank = wanted // slot_count
    slot_within = wanted % slot_count
    chosen = jnp.logical_and(
        (owner_rank == my_replica)[:, :, None],
        slot_within[:, :, None] == jnp.arange(slot_count, dtype=jnp.int32)[None, None, :],
    ).astype(jnp.bfloat16)
    send_wide = jnp.einsum(
        "dws,sx->dwx",
        chosen,
        store_wide[0].reshape(slot_count, wide_span),
        preferred_element_type=jnp.float32,
    ).astype(jnp.bfloat16)
    send_narrow = jnp.einsum(
        "dws,sx->dwx",
        chosen,
        store_narrow[0].reshape(slot_count, narrow_span),
        preferred_element_type=jnp.float32,
    ).astype(jnp.bfloat16)
    got_wide, got_narrow = (
        lax.all_to_all(send_wide, "replica", split_axis=0, concat_axis=0, tiled=True),
        lax.all_to_all(send_narrow, "replica", split_axis=0, concat_axis=0, tiled=True),
    )
    fetched_wide = jnp.sum(got_wide.astype(jnp.float32), axis=0).astype(jnp.bfloat16)
    fetched_narrow = jnp.sum(got_narrow.astype(jnp.float32), axis=0).astype(jnp.bfloat16)
    fetched_wide = fetched_wide.reshape(2, 2, rank_count, local_width)
    fetched_narrow = fetched_narrow.reshape(2, 2, rank_count, narrow_width)
    full_wide = lax.all_gather(fetched_wide, "tensor", axis=3, tiled=True)
    query_down = full_wide[:, 0]
    output_up = full_wide[:, 1]
    query_up = fetched_narrow[:, 0]
    output_down = fetched_narrow[:, 1]
    weight_query = (
        merged_query[0].astype(jnp.float32)
        + adapter_scale * outer_product(query_down[1], query_up[1])
        - adapter_scale * outer_product(query_down[0], query_up[0])
    ).astype(jnp.bfloat16)
    weight_output = (
        merged_output[0].astype(jnp.float32)
        + adapter_scale * outer_product(output_down[1], output_up[1])
        - adapter_scale * outer_product(output_down[0], output_up[0])
    ).astype(jnp.bfloat16)
    step_count = tokens.shape[1]
    positions = jnp.arange(key_cache.shape[3], dtype=jnp.int32)
    outputs = []
    for step_number in range(step_count):
        slab_piece = lax.all_gather(tokens[:, step_number], "tensor", axis=2, tiled=True)
        projected = jnp.dot(
            slab_piece.reshape(-1, slab_piece.shape[-1]),
            weight_query,
            preferred_element_type=jnp.float32,
        )
        visible = positions[None, :] < (context_length[0] + step_number)[:, None]
        contexts = attend(
            projected.astype(jnp.bfloat16), key_cache[0, 0], value_cache[0, 0], visible
        )
        partial_sum = jnp.dot(contexts, weight_output, preferred_element_type=jnp.float32)
        outputs.append(
            lax.psum_scatter(
                partial_sum.astype(jnp.bfloat16), "tensor", scatter_dimension=1, tiled=True
            )
        )
    return jnp.stack(outputs, 0)[None]


def solution(mesh):
    return jax.shard_map(
        on_device,
        mesh=mesh,
        in_specs=(
            P(("group", "replica"), None, None, "tensor"),
            P(("group", "replica"), None, "tensor"),
            P(("group", "replica"), "tensor", None),
            P(("group", "replica"), None, None, None, "tensor"),
            P(("group", "replica"), None, None, None, "tensor"),
            P(("group", "replica"), "tensor", None, None, None),
            P(("group", "replica"), "tensor", None, None, None),
            P(("group", "replica"), None),
            P("group"),
            P("group"),
            P("group"),
        ),
        out_specs=P(("group", "replica"), None, None, "tensor"),
        check_vma=False,
    )
```

profile of v0, /device:TPU:0, one launch (start us, length us, event | category | flops | bytes accessed | tf_op | source)
XLA Modules:
  0.0 320.3 jit_solution(11690659878135501873)
XLA Ops:
  6.6 4.0 %reshape.243 = bf16[8,131072,1]{1,0,2:T(8,128)(2,1)} reshape(bf16[1,8,2,32,2048]{4,3,2,1,0:T(8,128)(2,1)} %param.14) | data formatting | bytes 4194304 | tf_op jit(solution)/shard_map/reshape;squeeze | solution.py:62
  10.6 0.6 gather_fusion.1
  11.3 0.6 gather_fusion
  11.9 2.4 convolution_convert_fusion
  14.4 2.2 copy.16
  16.5 29.8 %all_to_all.10 = bf16[4,2,131072]{2,1,0:T(2,128)(2,1)} all-to-all(bf16[4,2,131072]{2,1,0:T(2,128)(2,1)S(1)} %copy.16), channel_id=1, replica_groups=mesh['group'=2,'replica'=4,'tensor'=4] {'replica'}, dimensions={0} | all-to-all | bytes 4194304 | tf_op jit(solution)/shard_map/all_to_all | solution.py:72
  46.3 4.1 %reduce_sum.42 = bf16[2,131072]{1,0:T(2,128)(2,1)S(1)} reduce(bf16[4,2,131072]{2,1,0:T(2,128)(2,1)} %all_to_all.10, bf16[]{:T(256)} %constant.44.clone.1), dimensions={0}, to_apply=%region_0.1 | reduce | flops 786432 | bytes 2621442 | tf_op jit(solution)/shard_map/reduce_sum | solution.py:75
  50.5 1.0 copy.20
  51.4 0.0 all-gather.6.cloned.1.call-update
  51.5 0.0 all-gather.10.cloned.1.call-start
  51.5 1.1 fusion.68
  52.6 0.0 all-gather.10.cloned.1.call-update
  52.6 1.7 reshape.244
  54.3 0.5 convolution_convert_fusion.1
  54.9 2.0 copy.17
  56.9 3.5 %all-to-all-start.1 = ((bf16[4,2,65536]{2,1,0:T(2,128)(2,1)}), bf16[4,2,65536]{2,1,0:T(2,128)(2,1)S(1)}, u32[]{:S(2)}, u32[]{:S(2)}) async-start(bf16[4,2,65536]{2,1,0:T(2,128)(2,1)} %copy.17), calls=%async_computation.1 | async-start | bytes 2097152 | tf_op jit(solution)/shard_map/all_to_all | solution.py:73
  60.5 0.0 all-gather.8.cloned.1.call-start
  60.5 0.7 all-gather.8.cloned.1.call-update
  61.2 0.3 reduce-scatter.5.cloned.1.call-start
  61.5 0.1 iota_compare_fusion
  61.6 13.3 %all-to-all-done.1 = bf16[4,2,65536]{2,1,0:T(2,128)(2,1)S(1)} async-done(((bf16[4,2,65536]{2,1,0:T(2,128)(2,1)}), bf16[4,2,65536]{2,1,0:T(2,128)(2,1)S(1)}, u32[]{:S(2)}, u32[]{:S(2)}) %all-to-all-start.1) | async-done | bytes 1048608 | tf_op jit(solution)/shard_map/all_to_all | solution.py:73
  74.9 1.5 reduce_sum.43
  76.4 22.0 %all-gather.6.cloned.1.call-done = bf16[2,2,32,8192]{3,2,1,0:T(8,128)(2,1)} async-done(((bf16[2,2,32,2048]{3,2,1,0:T(8,128)(2,1)}), bf16[2,2,32,8192]{3,2,1,0:T(8,128)(2,1)}) %all-gather.6.cloned.1.call-update) | async-done | bytes 2097168 | tf_op jit(solution)/shard_map/all_gather | solution.py:79
  98.5 14.7 %fusion.53 = f32[8192,1024]{1,0:T(8,128)} fusion(bf16[2,2,32,8192]{3,2,1,0:T(8,128)(2,1)} %all-gather.6.cloned.1.call-done, bf16[2,2,32,1024]{3,2,1,0:T(8,128)(2,1)S(1)} %bitcast.116), kind=kOutput, calls=%fused_computation.46 | convolution fusion | flops 536870912 | bytes 34144256 | tf_op jit(solution)/shard_map/dot_general | solution.py:10
  113.2 24.4 %fusion.5 = bf16[8192,1024]{1,0:T(8,128)(2,1)} fusion(f32[8192,1024]{1,0:T(8,128)} %fusion.53, bf16[1,8192,1024]{2,1,0:T(8,128)(2,1)} %param.12, bf16[2,2,32,8192]{3,2,1,0:T(8,128)(2,1)} %all-gather.6.cloned.1.call-done, bf16[2,2,32,1024]{3,2,1,0:T(8,128)(2,1)S(1)} %bitcast.117), kind=kOutput, calls=%fused_computation.11 | convolution fusion | flops 587202560 | bytes 67698688 | tf_op jit(solution)/shard_map/dot_general | solution.py:10
  137.6 7.1 %all-gather.10.cloned.1.call-done = bf16[1,1,128,8192]{3,2,1,0:T(8,128)(2,1)} async-done(((bf16[1,1,128,2048]{3,2,1,0:T(8,128)(2,1)}), bf16[1,1,128,8192]{3,2,1,0:T(8,128)(2,1)}) %all-gather.10.cloned.1.call-update) | async-done | bytes 2097168 | tf_op jit(solution)/shard_map/all_gather | solution.py:98
  144.7 11.6 %fusion.49 = bf16[1024,128]{1,0:T(8,128)(2,1)} fusion(bf16[8192,1024]{1,0:T(8,128)(2,1)} %fusion.5, bf16[1,1,128,8192]{3,2,1,0:T(8,128)(2,1)} %all-gather.10.cloned.1.call-done), kind=kOutput, calls=%fused_computation.39 | convolution fusion | flops 2147614720 | bytes 19136512 | tf_op jit(solution)/shard_map/dot_general | solution.py:99
  156.3 1.8 copy.19
  158.1 1.9 fusion.34
  160.0 0.8 copy-done.3
  160.8 0.3 fusion.69
  161.2 3.8 %fusion.43 = bf16[128,8,128]{2,1,0:T(8,128)(2,1)} fusion(bf16[1,1,128,48,128]{4,3,2,1,0:T(8,128)(2,1)S(1)} %copy-done, f32[8,128]{0,1:T(8,128)S(1)} %fusion.69, f32[8,128,48]{2,0,1:T(8,128)} %copy-done.3), kind=kOutput, calls=%fused_computation.37 | convolution fusion | flops 12862511 | bytes 2035712 | tf_op jit(solution)/shard_map/qrc,rcd->rqd/dot_general | solution.py:26
  165.0 24.7 %fusion.52 = f32[1024,8192]{1,0:T(8,128)} fusion(bf16[2,2,32,8192]{3,2,1,0:T(8,128)(2,1)} %all-gather.6.cloned.1.call-done, bf16[2,2,32,1024]{3,2,1,0:T(8,128)(2,1)S(1)} %bitcast.118), kind=kOutput, calls=%fused_computation.43 | convolution fusion | flops 536870912 | bytes 34144256 | tf_op jit(solution)/shard_map/dot_general | solution.py:10
  189.7 23.8 %fusion.3 = bf16[1024,8192]{1,0:T(8,128)(2,1)} fusion(f32[1024,8192]{1,0:T(8,128)} %fusion.52, bf16[1,1024,8192]{2,1,0:T(8,128)(2,1)} %param.13, bf16[2,2,32,8192]{3,2,1,0:T(8,128)(2,1)} %all-gather.6.cloned.1.call-done, bf16[2,2,32,1024]{3,2,1,0:T(8,128)(2,1)S(1)} %bitcast.119), kind=kOutput, calls=%fused_computation.8 | convolution fusion | flops 587202560 | bytes 67698688 | tf_op jit(solution)/shard_map/dot_general | solution.py:10
  213.5 9.6 %convolution_convert_fusion.2 = bf16[128,8192]{1,0:T(8,128)(2,1)} fusion(bf16[1024,8192]{1,0:T(8,128)(2,1)} %fusion.3, bf16[16,8,8,128]{3,2,1,0:T(8,128)(2,1)} %bitcast.123), kind=kOutput, calls=%fused_computation.12 | convolution fusion | flops 2148532224 | bytes 19136512 | tf_op jit(solution)/shard_map/dot_general | solution.py:108
  223.1 0.0 reduce-scatter.3.cloned.1.call-start
  223.2 0.1 iota_compare_fusion.1
  223.2 0.0 all-gather.8.cloned.1.call-done
  223.3 12.0 %fusion.46 = bf16[1024,128]{1,0:T(8,128)(2,1)} fusion(bf16[8192,1024]{1,0:T(8,128)(2,1)} %fusion.5, bf16[1,1,128,8192]{3,2,1,0:T(8,128)(2,1)} %all-gather.8.cloned.1.call-done), kind=kOutput, calls=%fused_computation.38 | convolution fusion | flops 2147614720 | bytes 19136512 | tf_op jit(solution)/shard_map/dot_general | solution.py:99
  235.3 1.1 copy.18
  236.4 0.9 fusion.37
  237.3 0.8 copy-done.4
  238.1 0.3 fusion.70
  238.5 3.1 fusion.40
  241.6 9.5 %convolution_convert_fusion.3 = bf16[128,8192]{1,0:T(8,128)(2,1)} fusion(bf16[1024,8192]{1,0:T(8,128)(2,1)} %fusion.3, bf16[16,8,8,128]{3,2,1,0:T(8,128)(2,1)S(1)} %bitcast.124), kind=kOutput, calls=%fused_computation.13 | convolution fusion | flops 2148532224 | bytes 19136512 | tf_op jit(solution)/shard_map/dot_general | solution.py:108
  251.2 14.7 %reduce-scatter.5.cloned.1.call-done = bf16[128,2048]{1,0:T(8,128)(2,1)} async-done(((bf16[128,8192]{1,0:T(8,128)(2,1)}), bf16[128,2048]{1,0:T(8,128)(2,1)}) %reduce-scatter.5.cloned.1.call-update) | async-done | bytes 524304 | tf_op jit(solution)/shard_map/reduce_scatter | solution.py:110
  265.8 45.5 %reduce-scatter.3.cloned.1.call-done = bf16[128,2048]{1,0:T(8,128)(2,1)} async-done(((bf16[128,8192]{1,0:T(8,128)(2,1)}), bf16[128,2048]{1,0:T(8,128)(2,1)}) %reduce-scatter.3.cloned.1.call-update) | async-done | bytes 524304 | tf_op jit(solution)/shard_map/reduce_scatter | solution.py:110
  311.3 2.3 maximum_bitcast_fusion
  (27 shorter events, 0.2 us)
Async XLA Ops:
  6.5 154.6 %copy-start = (bf16[1,1,128,48,128]{4,3,2,1,0:T(8,128)(2,1)S(1)}, bf16[1,1,128,48,128]{4,3,2,1,0:T(8,128)(2,1)}, u32[]{:S(2)}) copy-start(bf16[1,1,128,48,128]{4,3,2,1,0:T(8,128)(2,1)} %param.17) | copy-start | bytes 4718596
  6.5 91.9 %all-gather.6.cloned.1.call-start = ((), (), s32[]{:S(2)}) async-start(), calls=%async_computation.4 | async-start | bytes 2621440 | tf_op jit(solution)/shard_map/all_gather | solution.py:79
  6.5 4.0 %copy-start.7 = (s32[4]{0:T(128)S(1)}, s32[4]{0:T(128)}, u32[]{:S(2)}) copy-start(s32[4]{0:T(128)} %param.21) | copy-start | bytes 52
  6.5 4.0 %copy-start.8 = (s32[4]{0:T(128)S(1)}, s32[4]{0:T(128)}, u32[]{:S(2)}) copy-start(s32[4]{0:T(128)} %param.20) | copy-start | bytes 52
  6.5 4.1 %copy-start.1 = (s32[16]{0:T(128)S(1)}, s32[16]{0:T(128)}, u32[]{:S(2)}) copy-start(s32[16]{0:T(128)} %param.19) | copy-start | bytes 196
  46.3 5.2 %copy-start.5 = (bf16[1,2,128,2048]{3,2,1,0:T(8,128)(2,1)S(1)}, bf16[1,2,128,2048]{3,2,1,0:T(8,128)(2,1)}, u32[]{:S(2)}) copy-start(bf16[1,2,128,2048]{3,2,1,0:T(8,128)(2,1)} %param.11) | copy-start | bytes 3145732
  51.5 93.2 %all-gather.10.cloned.1.call-start = ((), (), s32[]{:S(2)}) async-start(), calls=%async_computation.8 | async-start | bytes 2621440 | tf_op jit(solution)/shard_map/all_gather | solution.py:98
  54.9 6.6 %copy-start.6 = (s32[1,128]{1,0:T(1,128)S(1)}, s32[1,128]{1,0:T(1,128)}, u32[]{:S(2)}) copy-start(s32[1,128]{1,0:T(1,128)} %param.18) | copy-start | bytes 1540
  56.9 18.0 %all-to-all-start.1 = ((bf16[4,2,65536]{2,1,0:T(2,128)(2,1)}), bf16[4,2,65536]{2,1,0:T(2,128)(2,1)S(1)}, u32[]{:S(2)}, u32[]{:S(2)}) async-start(bf16[4,2,65536]{2,1,0:T(2,128)(2,1)} %copy.17), calls=%async_computation.1 | async-start | bytes 2097152 | tf_op jit(solution)/shard_map/all_to_all | solution.py:73
  60.5 162.8 %all-gather.8.cloned.1.call-start = ((), (), s32[]{:S(2)}) async-start(), calls=%async_computation.7 | async-start | bytes 2621440 | tf_op jit(solution)/shard_map/all_gather | solution.py:98
  61.2 204.6 %reduce-scatter.5.cloned.1.call-start = ((), (), s32[]{:S(2)}) async-start(), calls=%async_computation.6 | async-start | bytes 2621440 | tf_op jit(solution)/shard_map/reduce_scatter | solution.py:110
  137.6 20.5 %copy-start.2 = (bf16[1,1,128,48,128]{4,3,2,1,0:T(8,128)(2,1)S(1)}, bf16[1,1,128,48,128]{4,3,2,1,0:T(8,128)(2,1)}, u32[]{:S(2)}) copy-start(bf16[1,1,128,48,128]{4,3,2,1,0:T(8,128)(2,1)} %param.16) | copy-start | bytes 4718596
  160.0 0.8 copy-start.3
  223.1 88.2 %reduce-scatter.3.cloned.1.call-start = ((), (), s32[]{:S(2)}) async-start(), calls=%async_computation.5 | async-start | bytes 2621440 | tf_op jit(solution)/shard_map/reduce_scatter | solution.py:110
  237.3 0.8 copy-start.4
Sparse Core Ops, SparseCore 0:
  51.6 46.8 all-gather.5
  100.0 44.6 all-gather.9
  146.3 44.6 all-gather.7
  223.2 42.5 reduce-scatter.4
  268.1 43.1 reduce-scatter.2
where the time goes:
time: 323 us; the launch traced here: 320 us
  matrix products  143 us (44%)
  waiting for transfers between devices  103 us (32%)
  blocking collectives  29.8 us (9%)
  local copies, waits for them, and re-layouts  17.9 us (6%)
  between operations  13.5 us (4%)
  other arithmetic  8.8 us (3%)
  starting transfers between devices  3.95 us (1%)
    dot_general x4, matrix products, outer_product(): lax.dot_general(left_factor, right_factor, (((0,), (0,)), ((), ())), pref...  87.7 us
    reduce_scatter x2, waiting for transfers between devices, on_device(): lax.psum_scatter(partial_sum.astype(jnp.bfloat16), 'tensor', scatter_dime...  60.2 us
    all_to_all x1, blocking collectives, on_device(): lax.all_to_all(send_wide, 'replica', split_axis=0, concat_axis=0, tiled=T...  29.8 us
    dot_general x2, matrix products, on_device(): jnp.dot(slab_piece.reshape(-1, slab_piece.shape[-1]), weight_query, prefe...  23.6 us
    all_gather x1, waiting for transfers between devices, on_device(): full_wide = lax.all_gather(fetched_wide, 'tensor', axis=3, tiled=True)  22 us
    dot_general x2, matrix products, on_device(): jnp.dot(contexts, weight_output, preferred_element_type=jnp.float32)  19.1 us
    all_to_all x1, waiting for transfers between devices, on_device(): lax.all_to_all(send_narrow, 'replica', split_axis=0, concat_axis=0, tiled...  13.3 us
    all_gather x2, waiting for transfers between devices, on_device(): lax.all_gather(tokens[:, step_number], 'tensor', axis=2, tiled=True)  7.14 us
  transfers between devices with their start and end apart: 6, of which 5 were waited for; matrix products, arithmetic and copies ran while one was open for 47% of the time, Pallas kernels for 0%

commit v1 on v0

v1 whole, which is shorter than its diff:
```python
import functools

import jax
import jax.numpy as jnp
from jax import lax
from jax.experimental import pallas as pl
from jax.experimental.pallas import tpu as pltpu
from jax.sharding import PartitionSpec as P

adapter_scale = 0.25
CHUNKS = 4
GROUP = 8
MESH = pl.DeviceIdType.MESH
F32 = jnp.float32
BF16 = jnp.bfloat16


def nt_dot(left, right):
    return lax.dot_general(left, right, (((1,), (1,)), ((), ())), preferred_element_type=F32)


def kernel(
    n, nr, steps, rows, width, narrow, head_size, ctx, slots, rank,
    owner_ref, old_ref, new_ref, upper_ref,
    tokens_hbm, wq_hbm, wo_hbm, wide_hbm, narrow_hbm, key_hbm, value_hbm,
    out_ref,
    wq, wo, wide, nar, key, value, tok, part, qacc, ctxs, total,
    send_ad, recv_ad, ad, zbuf, ybuf,
    wq_sem, wo_sem, store_sem, kv_sem, tok_sem,
    ag_send, ag_recv, rs_send, rs_recv, ad_send, ad_recv, z_send, z_recv, y_send, y_recv,
):
    z = lax.axis_index("tensor")
    me_r = lax.axis_index("replica")
    chunk_rows = rows // CHUNKS
    chunk = steps * chunk_rows
    heads = narrow // head_size
    keys = GROUP * ctx

    def token_copy(c, s):
        return pltpu.make_async_copy(
            tokens_hbm.at[s, pl.ds(c * chunk_rows, chunk_rows)],
            tok.at[c, z, pl.ds(s * chunk_rows, chunk_rows)],
            tok_sem.at[c, s],
        )

    for c in range(CHUNKS):
        for s in range(steps):
            token_copy(c, s).start()
    wide_copy = pltpu.make_async_copy(wide_hbm, wide, store_sem.at[0])
    nar_copy = pltpu.make_async_copy(narrow_hbm, nar, store_sem.at[1])
    wide_copy.start()
    nar_copy.start()

    def wq_copy(b):
        return pltpu.make_async_copy(wq_hbm.at[b], wq.at[b], wq_sem.at[b])

    def wo_copy(b):
        return pltpu.make_async_copy(
            wo_hbm.at[:, pl.ds(b * width, width)], wo.at[b], wo_sem.at[b]
        )

    for b in range(n):
        wq_copy(b).start()
    key_copy = pltpu.make_async_copy(key_hbm, key, kv_sem.at[0])
    value_copy = pltpu.make_async_copy(value_hbm, value, kv_sem.at[1])
    key_copy.start()
    value_copy.start()
    for b in range(n):
        wo_copy(b).start()

    barrier = pltpu.get_barrier_semaphore()

    @pl.loop(1, n)
    def _(k):
        pl.semaphore_signal(barrier, inc=1, device_id={"tensor": lax.rem(z + k, n)}, device_id_type=MESH)

    @pl.loop(1, nr)
    def _(k):
        pl.semaphore_signal(barrier, inc=1, device_id={"replica": lax.rem(me_r + k, nr)}, device_id_type=MESH)

    pl.semaphore_wait(barrier, n - 1 + nr - 1)

    def ag_copy(c, b, way):
        return pltpu.make_async_remote_copy(
            src_ref=tok.at[c, b], dst_ref=tok.at[c, b],
            send_sem=ag_send.at[c, b, way], recv_sem=ag_recv.at[c, b],
            device_id={"tensor": z + 1 if way == 0 else z - 1}, device_id_type=MESH,
        )

    for c in range(CHUNKS):
        for s in range(steps):
            token_copy(c, s).wait()

    def send_own(c):
        @pl.when(z < n - 1)
        def _():
            ag_copy(c, z, 0).start()

        @pl.when(z > 0)
        def _():
            ag_copy(c, z, 1).start()

    send_own(0)

    wide_copy.wait()
    nar_copy.wait()

    def ad_copy(side, j):
        return pltpu.make_async_remote_copy(
            src_ref=send_ad.at[side, j], dst_ref=recv_ad.at[side, me_r],
            send_sem=ad_send.at[side, j], recv_sem=ad_recv.at[side, me_r],
            device_id={"replica": j}, device_id_type=MESH,
        )

    def ad_arrival(side, j):
        return pltpu.make_async_remote_copy(
            src_ref=send_ad.at[side, j], dst_ref=recv_ad.at[side, j],
            send_sem=ad_send.at[side, j], recv_sem=ad_recv.at[side, j],
            device_id={"replica": j}, device_id_type=MESH,
        )

    for side in range(2):
        @pl.loop(1, nr + 1)
        def _(k, side=side):
            j = lax.rem(me_r + k, nr)
            for w, tenant_ref in ((0, old_ref), (1, new_ref)):
                place = owner_ref[tenant_ref[j]]
                mine = (place // slots == me_r).astype(F32)
                slot = place % slots
                spot = pl.ds(w * rank, rank)
                send_ad[side, j, spot, 0:width] = (wide[slot, side].astype(F32) * mine).astype(BF16)
                send_ad[side, j, spot, width:] = (nar[slot, side].astype(F32) * mine).astype(BF16)

            @pl.when(k < nr)
            def _():
                ad_copy(side, j).start()

    def take_adapter(side):
        ad[side, 0:2 * rank] = send_ad[side, me_r]
        ad[side, 2 * rank:] = jnp.zeros_like(ad[side, 2 * rank:])

        @pl.loop(1, nr)
        def _(k):
            j = lax.rem(me_r + k, nr)
            ad_arrival(side, j).wait_recv()
            ad[side, 0:2 * rank] += recv_ad[side, j]

    lane = lax.broadcasted_iota(jnp.int32, (chunk, 128), 1)
    factor = jnp.where(lane < rank, -adapter_scale, adapter_scale).astype(F32)

    def low_rank(pieces, matrix):
        mixed = pieces * factor
        high = mixed.astype(BF16)
        low = (mixed - high.astype(F32)).astype(BF16)
        return (
            jnp.dot(high, matrix, preferred_element_type=F32)
            + jnp.dot(low, matrix, preferred_element_type=F32)
        )

    def z_copy(peer):
        return pltpu.make_async_remote_copy(
            src_ref=zbuf.at[z], dst_ref=zbuf.at[z], send_sem=z_send.at[peer],
            recv_sem=z_recv.at[z], device_id={"tensor": peer}, device_id_type=MESH,
        )

    def z_arrival(peer):
        return pltpu.make_async_remote_copy(
            src_ref=zbuf.at[peer], dst_ref=zbuf.at[peer], send_sem=z_send.at[peer],
            recv_sem=z_recv.at[peer], device_id={"tensor": peer}, device_id_type=MESH,
        )

    def y_copy(c, peer):
        return pltpu.make_async_remote_copy(
            src_ref=ybuf.at[c, z], dst_ref=ybuf.at[c, z], send_sem=y_send.at[c, peer],
            recv_sem=y_recv.at[c, z], device_id={"tensor": peer}, device_id_type=MESH,
        )

    def y_arrival(c, peer):
        return pltpu.make_async_remote_copy(
            src_ref=ybuf.at[c, peer], dst_ref=ybuf.at[c, peer], send_sem=y_send.at[c, peer],
            recv_sem=y_recv.at[c, peer], device_id={"tensor": peer}, device_id_type=MESH,
        )

    q_tile = min(narrow, 512)
    o_tile = min(width, 512)

    def project(c, b, first):
        @pl.when(c == 0)
        def _():
            wq_copy(b).wait()

        @pl.loop(0, narrow // q_tile)
        def _(t):
            cols = pl.ds(pl.multiple_of(t * q_tile, q_tile), q_tile)
            product = jnp.dot(tok[c, b], wq[b, :, cols], preferred_element_type=F32)
            if first:
                qacc[:, cols] = product
            else:
                qacc[:, cols] += product

    def rs_copy(c, b, source, way):
        slot = b if way == 0 else jnp.where(b == z - 1, n, b)
        return pltpu.make_async_remote_copy(
            src_ref=source.at[c, b], dst_ref=part.at[c, slot],
            send_sem=rs_send.at[c, b], recv_sem=rs_recv.at[c, slot],
            device_id={"tensor": z + 1 if way == 0 else z - 1}, device_id_type=MESH,
        )

    def rs_arrival(c, slot):
        return pltpu.make_async_remote_copy(
            src_ref=part.at[c, slot], dst_ref=part.at[c, slot],
            send_sem=rs_send.at[c, 0], recv_sem=rs_recv.at[c, slot],
            device_id={"tensor": lax.rem(z + 1, n)}, device_id_type=MESH,
        )

    def rs_pass(c, b, way):
        rs_arrival(c, b).wait_recv()
        part[c, b] = (part[c, b].astype(F32) + tok[c, b].astype(F32)).astype(BF16)
        rs_copy(c, b, part, way).start()

    def rs_step(c, i):
        far = n - 1 - i

        @pl.when(jnp.logical_and(z > 0, far > z))
        def _():
            rs_pass(c, far, 0)

        @pl.when(jnp.logical_and(z < n - 1, i < z))
        def _():
            rs_pass(c, i, 1)

    def finish(c):
        @pl.loop(1, n)
        def _(k):
            y_arrival(c, lax.rem(z + k, n)).wait_recv()

        mixed = ybuf[c, 0].astype(F32)
        for b in range(1, n):
            mixed = mixed + ybuf[c, b].astype(F32)
        total[...] = tok[c, z].astype(F32) + low_rank(mixed, ad[1, :, 0:width])

        @pl.when(z > 0)
        def _():
            rs_arrival(c, z).wait_recv()
            total[...] += part[c, z].astype(F32)

        @pl.when(z < n - 1)
        def _():
            rs_arrival(c, n).wait_recv()
            total[...] += part[c, n].astype(F32)

        for s in range(steps):
            out_ref[s, pl.ds(pl.multiple_of(c * chunk_rows, chunk_rows), chunk_rows)] = total[
                s * chunk_rows:(s + 1) * chunk_rows
            ].astype(BF16)

    def attention(c):
        queries_in_group = heads * steps * GROUP
        row = lax.broadcasted_iota(jnp.int32, (queries_in_group, keys), 0)
        column = lax.broadcasted_iota(jnp.int32, (queries_in_group, keys), 1)
        lowest = (row % GROUP) * ctx

        @pl.loop(0, chunk_rows // GROUP)
        def _(g):
            place = c * (chunk_rows // GROUP) + g

            def spot(s):
                return pl.ds(pl.multiple_of(s * chunk_rows + g * GROUP, GROUP), GROUP)

            pieces = [
                qacc[spot(s), h * head_size:(h + 1) * head_size]
                for h in range(heads) for s in range(steps)
            ]
            queries = jnp.concatenate(pieces, axis=0).astype(BF16)
            scores = nt_dot(queries, key[place]) * head_size ** (-0.5)
            visible = jnp.logical_and(column >= lowest, column < upper_ref[place])
            scores = jnp.where(visible, scores, -1e30)
            highest = jnp.max(scores, axis=1, keepdims=True)
            weights = jnp.exp(scores - highest)
            weights = jnp.where(visible, weights, 0.0)
            probability = (weights / jnp.sum(weights, axis=1, keepdims=True)).astype(BF16)
            blended = jnp.dot(probability, value[place], preferred_element_type=F32)
            index = 0
            for h in range(heads):
                for s in range(steps):
                    ctxs[spot(s), h * head_size:(h + 1) * head_size] = blended[
                        index * GROUP:(index + 1) * GROUP
                    ]
                    index += 1

    @pl.loop(0, CHUNKS)
    def _(c):
        @pl.when(c + 1 < CHUNKS)
        def _():
            send_own(c + 1)

        project(c, z, True)

        @pl.loop(1, n)
        def _(d):
            left, right = z - d, z + d

            @pl.when(left >= 0)
            def _():
                ag_copy(c, left, 1).wait_recv()

                @pl.when(z < n - 1)
                def _():
                    ag_copy(c, left, 0).start()

            @pl.when(right < n)
            def _():
                ag_copy(c, right, 0).wait_recv()

                @pl.when(z > 0)
                def _():
                    ag_copy(c, right, 1).start()

            @pl.when(c > 0)
            def _():
                rs_step(c - 1, d - 1)

            @pl.when(left >= 0)
            def _():
                project(c, left, False)

            @pl.when(right < n)
            def _():
                project(c, right, False)

        @pl.when(c == 0)
        def _():
            take_adapter(0)
            for k in range(CHUNKS):
                zbuf[z, k * chunk:(k + 1) * chunk] = nt_dot(tok[k, z], ad[0, :, 0:width]).astype(BF16)

            @pl.loop(1, n)
            def _(k):
                z_copy(lax.rem(z + k, n)).start()

            take_adapter(1)
            key_copy.wait()
            value_copy.wait()

            @pl.loop(1, n)
            def _(k):
                z_arrival(lax.rem(z + k, n)).wait_recv()

        mine = pl.ds(pl.multiple_of(c * chunk, chunk), chunk)
        mixed = zbuf[0, mine].astype(F32)
        for b in range(1, n):
            mixed = mixed + zbuf[b, mine].astype(F32)
        qacc[...] += low_rank(mixed, ad[0, :, width:])
        attention(c)
        contexts = ctxs[...].astype(BF16)
        ybuf[c, z] = nt_dot(contexts, ad[1, :, width:]).astype(BF16)

        @pl.loop(1, n)
        def _(k):
            y_copy(c, lax.rem(z + k, n)).start()

        @pl.loop(0, n)
        def _(b):
            @pl.when(jnp.logical_and(z < n - 1, b <= z))
            def _():
                ag_copy(c, b, 0).wait_send()

            @pl.when(jnp.logical_and(z > 0, b >= z))
            def _():
                ag_copy(c, b, 1).wait_send()

        @pl.loop(0, n)
        def _(i):
            b = jnp.where(i % 2 == 0, n - 1 - i // 2, i // 2)

            @pl.when(c == 0)
            def _():
                wo_copy(b).wait()

            @pl.loop(0, width // o_tile)
            def _(t):
                cols = pl.ds(pl.multiple_of(t * o_tile, o_tile), o_tile)
                tok[c, b, :, cols] = jnp.dot(
                    ctxs[...].astype(BF16), wo[b, :, cols], preferred_element_type=F32
                ).astype(BF16)

            @pl.when(jnp.logical_and(z == 0, b > 0))
            def _():
                rs_copy(c, b, tok, 0).start()

            @pl.when(jnp.logical_and(z == n - 1, b < n - 1))
            def _():
                rs_copy(c, b, tok, 1).start()

        @pl.when(c > 0)
        def _():
            finish(c - 1)

    @pl.loop(0, n - 1)
    def _(i):
        rs_step(CHUNKS - 1, i)

    finish(CHUNKS - 1)

    @pl.loop(1, n)
    def _(k):
        peer = lax.rem(z + k, n)
        z_copy(peer).wait_send()

        @pl.loop(0, CHUNKS)
        def _(c):
            y_copy(c, peer).wait_send()
            rs_copy(c, peer, part, 0).wait_send()

    @pl.loop(1, nr)
    def _(k):
        j = lax.rem(me_r + k, nr)
        for side in range(2):
            ad_copy(side, j).wait_send()


def on_device(
    tokens, merged_query, merged_output, store_wide, store_narrow,
    key_cache, value_cache, context_length, owner_slot, old_tenant, new_tenant,
):
    n, nr = lax.axis_size("tensor"), lax.axis_size("replica")
    steps, rows, width = tokens.shape[1:]
    narrow = merged_query.shape[2]
    slots, _, rank, _ = store_wide.shape[1:]
    ctx, head_size = key_cache.shape[3:]
    heads = narrow // head_size
    groups = rows // GROUP
    chunk_rows = rows // CHUNKS
    chunk = steps * chunk_rows
    upper = (
        context_length.reshape(groups, 1, 1, GROUP)
        + jnp.arange(steps, dtype=jnp.int32)[None, None, :, None]
        + ctx * jnp.arange(GROUP, dtype=jnp.int32)
    )
    upper = jnp.broadcast_to(upper, (groups, heads, steps, GROUP)).reshape(groups, -1, 1)
    hbm = pl.BlockSpec(memory_space=pl.ANY)
    smem = pl.BlockSpec(memory_space=pltpu.SMEM)
    vmem = pl.BlockSpec(memory_space=pltpu.VMEM)
    dma = pltpu.SemaphoreType.DMA
    result = pl.pallas_call(
        functools.partial(
            kernel, n, nr, steps, rows, width, narrow, head_size, ctx, slots, rank
        ),
        out_shape=jax.ShapeDtypeStruct((steps, rows, width), BF16),
        in_specs=[smem] * 3 + [vmem] + [hbm] * 7,
        out_specs=vmem,
        scratch_shapes=[
            pltpu.VMEM((n, width, narrow), BF16),
            pltpu.VMEM((n, narrow, width), BF16),
            pltpu.VMEM((slots, 2, rank, width), BF16),
            pltpu.VMEM((slots, 2, rank, narrow), BF16),
            pltpu.VMEM((groups, GROUP * ctx, head_size), BF16),
            pltpu.VMEM((groups, GROUP * ctx, head_size), BF16),
            pltpu.VMEM((CHUNKS, n, chunk, width), BF16),
            pltpu.VMEM((CHUNKS, n + 1, chunk, width), BF16),
            pltpu.VMEM((chunk, narrow), F32),
            pltpu.VMEM((chunk, narrow), F32),
            pltpu.VMEM((chunk, width), F32),
            pltpu.VMEM((2, nr, 2 * rank, width + narrow), BF16),
            pltpu.VMEM((2, nr, 2 * rank, width + narrow), BF16),
            pltpu.VMEM((2, 128, width + narrow), BF16),
            pltpu.VMEM((n, CHUNKS * chunk, 128), BF16),
            pltpu.VMEM((CHUNKS, n, chunk, 128), BF16),
            dma((n,)), dma((n,)), dma((2,)), dma((2,)), dma((CHUNKS, steps)),
            dma((CHUNKS, n, 2)), dma((CHUNKS, n)),
            dma((CHUNKS, n)), dma((CHUNKS, n + 1)),
            dma((2, nr)), dma((2, nr)),
            dma((n,)), dma((n,)), dma((CHUNKS, n)), dma((CHUNKS, n)),
        ],
        compiler_params=pltpu.CompilerParams(
            collective_id=0, has_side_effects=True, vmem_limit_bytes=63 * 2 ** 20
        ),
    )(
        owner_slot, old_tenant, new_tenant, upper,
        tokens[0], merged_query[0].reshape(n, width, narrow), merged_output[0],
        store_wide[0], store_narrow[0],
        key_cache[0, 0].reshape(groups, GROUP * ctx, head_size),
        value_cache[0, 0].reshape(groups, GROUP * ctx, head_size),
    )
    return result[None]


def solution(mesh):
    return jax.shard_map(
        on_device,
        mesh=mesh,
        in_specs=(
            P(("group", "replica"), None, None, "tensor"),
            P(("group", "replica"), None, "tensor"),
            P(("group", "replica"), "tensor", None),
            P(("group", "replica"), None, None, None, "tensor"),
            P(("group", "replica"), None, None, None, "tensor"),
            P(("group", "replica"), "tensor", None, None, None),
            P(("group", "replica"), "tensor", None, None, None),
            P(("group", "replica"), None),
            P("group"),
            P("group"),
            P("group"),
        ),
        out_specs=P(("group", "replica"), None, None, "tensor"),
        check_vma=False,
    )
```

time: 323 us -> 216 us (0.67)
  Pallas kernels: 0 us -> 209 us
  matrix products: 143 us -> 0 us
  waiting for transfers between devices: 103 us -> 0 us
  blocking collectives: 29.8 us -> 0 us
  between operations: 13.5 us -> 0.01 us
  local copies, waits for them, and re-layouts: 17.9 us -> 4.9 us
  other arithmetic: 8.8 us -> 1.39 us
  starting transfers between devices: 3.95 us -> 0 us
    pallas_call x0 -> x1, Pallas kernels: none -> 209 us  [on_device(): pl.pallas_call(functools.partial(kernel, n, nr, steps, rows, width, narro...]
    dot_general x14 -> x0, matrix products: 143 us -> none  [the longest x4 87.7 us: outer_product(): lax.dot_general(left_factor, right_factor, (((0,), (0,)), ((), ())), pref...]
    reduce_scatter x2 -> x0, waiting for transfers between devices: 60.2 us -> none  [on_device(): lax.psum_scatter(partial_sum.astype(jnp.bfloat16), 'tensor', scatter_dime...]
    all_to_all x1 -> x0, blocking collectives: 29.8 us -> none  [on_device(): lax.all_to_all(send_wide, 'replica', split_axis=0, concat_axis=0, tiled=T...]
    all_gather x3 -> x0, waiting for transfers between devices: 29.2 us -> none  [the longest x1 22 us: on_device(): full_wide = lax.all_gather(fetched_wide, 'tensor', axis=3, tiled=True)]
    all_to_all x1 -> x0, waiting for transfers between devices: 13.3 us -> none  [on_device(): lax.all_to_all(send_narrow, 'replica', split_axis=0, concat_axis=0, tiled...]
    another operation x2 -> x0, local copies, waits for them, and re-layouts: 5.71 us -> none  [the longest x1 4.01 us: on_device(): store_wide[0].reshape(slot_count, wide_span)]
    reduce_sum x2 -> x0, other arithmetic: 5.61 us -> none  [the longest x1 4.15 us: on_device(): jnp.sum(got_wide.astype(jnp.float32), axis=0).astype(jnp.bfloat16)]
  transfers between devices with their start and end apart: 6 -> 0, of which waited for: 5 -> 0; matrix products, arithmetic and copies ran while one was open for 47% -> 0% of each run, Pallas kernels for 0% -> 0%
where the time goes in v1:
time: 216 us
  Pallas kernels  209 us (97%)
  local copies, waits for them, and re-layouts  4.9 us (2%)
    pallas_call x1, Pallas kernels, on_device(): pl.pallas_call(functools.partial(kernel, n, nr, steps, rows, width, narro...  209 us

profile of v1, /device:TPU:0, one launch (start us, length us, event | category | flops | bytes accessed | tf_op | source)
XLA Modules:
  0.0 215.6 jit_solution(1470399045540969792)
XLA Ops:
  0.0 0.5 broadcast.27
  0.5 1.3 reduce.3
  1.8 0.1 add.33
  1.9 0.1 copy.12
  2.0 0.1 add_add_fusion
  2.1 1.9 copy.13.upper_ref
  4.0 209.3 %shard_map.109 = bf16[2,128,2048]{2,1,0:T(8,128)(2,1)} custom-call(s32[16]{0:T(128)} %owner_ref.1, s32[4]{0:T(128)} %old_ref.1, s32[4]{0:T(128)} %new_ref.1, s32[16,128,1]{2,1,0:T(8,128)} %copy.13.upper_ref, bf16[2,128,2048]{2,1,0:T(8,128)(2,1)} %bitcast.15, bf16[4,2048,1024]{2,1,0:T(8,128)(2,1)} %bitcast.9, bf16[1024,8192]{1,0:T(8,128)(2,1)} %bitcast.10, ...), custom_call_target="tpu_custom_call" | custom-call | tf_op jit(solution)/shard_map/pallas_call | solution.py:445
  213.3 2.3 %copy.15 = bf16[1,2,128,2048]{3,2,1,0:T(8,128)(2,1)} copy(bf16[1,2,128,2048]{3,2,1,0:T(8,128)(2,1)} %bitcast.11) | data formatting | bytes 2097152
  (2 shorter events, 0.0 us)
